TPU v7x, 32 devices: a whole 2x2x4 slice. The times are simulated.
32 devices in a mesh: groups: 2 (over y), tensor: 4 (over z), dp: 4 (over x, core).
Axes of the slice: x: 2, y: 2, z: 4, core: 2. Of those that a mesh axis runs over, the one named last changes fastest.
Arguments:
- inputs: bfloat16 [1536, 6144], P(('groups', 'tensor')), parts along dimension 0, may hold values from -36 to 36
- ln_gain: float32 [6144], replicated, may hold values from 0.25 to 1.75
- w_query: bfloat16 [6144, 512], P('dp', 'tensor'), may hold values from -0.078125 to 0.078125
- w_keyval: bfloat16 [4, 1536, 1024], P('dp', 'tensor'), may hold values from -0.078125 to 0.078125
- w_gate: bfloat16 [6144, 1536], P('dp', 'tensor'), may hold values from -0.078125 to 0.078125
- w_up: bfloat16 [6144, 1536], P('dp', 'tensor'), may hold values from -0.078125 to 0.078125
- w_out: bfloat16 [512, 6144], P('tensor', 'dp'), may hold values from -0.25 to 0.25
- w_down: bfloat16 [1536, 6144], P('tensor', 'dp'), may hold values from -0.15625 to 0.15625
- cache_keys: bfloat16 [8, 4, 256, 128], P(('groups', 'dp')), parts along dimension 0, may hold values from -500 to 500
- cache_values: bfloat16 [8, 4, 256, 128], P(('groups', 'dp')), parts along dimension 0, may hold values from -5 to 5
- lengths: int32 [8], P(('groups', 'dp')), parts along dimension 0, may hold values from 64 to 256, as said below
- starts: int32 [8], P(('groups', 'dp')), parts along dimension 0, may hold values from 64 to 511, as said below
Outputs:
- layer_out: bfloat16 [1536, 6144], P(('groups', 'tensor'), 'dp'), parts along dimension 0
There are 2 independent parts, one for each index of `groups`. A program takes and returns all parts, laid end to end along the dimension named above; an argument that names none is the same for every part. Nothing has to cross between parts.
Inputs may be any that keep to these rules, and one draw needn't show every extreme that they name: `lengths`: at most 256 live slots, and one sequence has exactly 256 in every draw. `starts`: a sequence's first new position is at least its number of live cache slots and less than that number plus 256; cached keys belong to earlier positions.
All inputs are finite; a program needn't handle non-finite values.
Results may differ from a plain program's by a relative error of at most 0.0054.
Values may be sent and summed in bfloat16 or wider, within the bound.
A program may use at most 64 MiB of HBM per device.

v0:
```python
import jax
import jax.numpy as jnp
from jax import lax
from jax.sharding import PartitionSpec as P

SPAN = 192


rope_base = 75000000.0
norm_eps = 1e-05


def layer_norm(row_values, gain_values):
    widened = row_values.astype(jnp.float32)
    centered = widened - jnp.mean(widened, axis=-1, keepdims=True)
    spread_sq = jnp.mean(centered * centered, axis=-1, keepdims=True)
    return (centered * lax.rsqrt(spread_sq + norm_eps) * gain_values).astype(jnp.bfloat16)


def rotate(values, positions):
    head_width = values.shape[-1]
    half_width = head_width // 2
    frequency = rope_base ** (-2.0 * jnp.arange(half_width, dtype=jnp.float32) / head_width)
    angles = positions[..., None] * frequency
    paired = values.reshape(values.shape[:-1] + (half_width, 2))
    even_part = paired[..., 0]
    odd_part = paired[..., 1]
    cosine = jnp.cos(angles)
    sine_vals = jnp.sin(angles)
    turned = jnp.stack(
        [even_part * cosine - odd_part * sine_vals, even_part * sine_vals + odd_part * cosine],
        axis=-1,
    )
    return turned.reshape(values.shape)


def on_device(
    inputs,
    ln_gain,
    w_query,
    w_keyval,
    w_gate,
    w_up,
    w_out,
    w_down,
    cache_keys,
    cache_values,
    lengths,
    starts,
):
    tensor_index = lax.axis_index("tensor")
    data_index = lax.axis_index("dp")
    tensor_count = lax.axis_size("tensor")
    block_width = w_gate.shape[0]
    sub_width = w_keyval.shape[1]
    head_width = w_query.shape[1]
    ffn_width = w_gate.shape[1]
    kv_heads = cache_keys.shape[1]
    kv_group = tensor_index // (tensor_count // kv_heads)
    normed = layer_norm(inputs, ln_gain)
    own_block = lax.dynamic_slice_in_dim(normed, data_index * block_width, block_width, 1)
    every_row = lax.all_gather(own_block, "tensor", axis=0, tiled=True)
    offsets = jnp.arange(SPAN, dtype=jnp.int32)
    positions = (starts[0] + offsets).astype(jnp.float32)
    kv_rows = lax.dynamic_slice_in_dim(every_row, tensor_index * sub_width, sub_width, 1)
    kv_term = jnp.dot(kv_rows, w_keyval[0], preferred_element_type=jnp.float32)
    keyval = lax.psum(kv_term, ("tensor", "dp"))
    own_keyval = lax.dynamic_slice_in_dim(keyval, data_index * SPAN, SPAN, 0)
    key_cols = lax.dynamic_slice_in_dim(own_keyval, kv_group * head_width, head_width, 1)
    value_cols = lax.dynamic_slice_in_dim(
        own_keyval, (kv_heads + kv_group) * head_width, head_width, 1
    )
    pieces = [
        jnp.dot(every_row, w_query, preferred_element_type=jnp.float32),
        jnp.dot(every_row, w_gate, preferred_element_type=jnp.float32),
        jnp.dot(every_row, w_up, preferred_element_type=jnp.float32),
    ]
    projected = lax.psum_scatter(
        jnp.concatenate(pieces, axis=1), "dp", scatter_dimension=0, tiled=True
    )
    query = projected[:, :head_width]
    gate_proj = projected[:, head_width : head_width + ffn_width]
    up_proj = projected[:, head_width + ffn_width : head_width + 2 * ffn_width]
    hidden_act = (jax.nn.silu(gate_proj) * up_proj).astype(jnp.bfloat16)
    rotated_query = rotate(query, positions).astype(jnp.bfloat16)
    new_keys = rotate(key_cols, positions).astype(jnp.bfloat16)
    new_values = value_cols.astype(jnp.bfloat16)
    cached_k = lax.dynamic_index_in_dim(cache_keys[0], kv_group, 0, keepdims=False)
    cached_v = lax.dynamic_index_in_dim(cache_values[0], kv_group, 0, keepdims=False)
    scale_factor = head_width ** (-0.5)
    cached_scores = (
        jnp.einsum("qd,kd->qk", rotated_query, cached_k, preferred_element_type=jnp.float32)
        * scale_factor
    )
    new_scores = (
        jnp.einsum("qd,kd->qk", rotated_query, new_keys, preferred_element_type=jnp.float32)
        * scale_factor
    )
    slot_index = jnp.arange(cached_k.shape[0], dtype=jnp.int32)
    cached_scores = jnp.where(slot_index[None, :] < lengths[0], cached_scores, -jnp.inf)
    causal = offsets[:, None] >= offsets[None, :]
    new_scores = jnp.where(causal, new_scores, -jnp.inf)
    row_peak = jnp.maximum(
        jnp.max(cached_scores, axis=-1, keepdims=True), jnp.max(new_scores, axis=-1, keepdims=True)
    )
    cached_exp = jnp.exp(cached_scores - row_peak)
    new_exp = jnp.exp(new_scores - row_peak)
    denominator = jnp.sum(cached_exp, axis=-1, keepdims=True) + jnp.sum(
        new_exp, axis=-1, keepdims=True
    )
    cached_prob = (cached_exp / denominator).astype(jnp.bfloat16)
    new_prob = (new_exp / denominator).astype(jnp.bfloat16)
    attended = (
        jnp.dot(cached_prob, cached_v, preferred_element_type=jnp.float32)
        + jnp.dot(new_prob, new_values, preferred_element_type=jnp.float32)
    ).astype(jnp.bfloat16)
    joined = jnp.concatenate([attended, hidden_act], axis=1)
    gathered_piece = lax.all_gather(joined, "dp", axis=0, tiled=True)
    partial_terms = jnp.dot(
        gathered_piece[:, :head_width], w_out, preferred_element_type=jnp.float32
    ) + jnp.dot(gathered_piece[:, head_width:], w_down, preferred_element_type=jnp.float32)
    row_share = inputs.shape[0]
    residual = lax.dynamic_slice_in_dim(inputs, data_index * block_width, block_width, 1).astype(
        jnp.float32
    )
    summed = lax.psum(partial_terms, "tensor")
    own_sum = lax.dynamic_slice_in_dim(summed, tensor_index * row_share, row_share, 0)
    return (residual + own_sum).astype(jnp.bfloat16)


def solution(mesh):
    return jax.shard_map(
        on_device,
        mesh=mesh,
        in_specs=(
            P(("groups", "tensor"), None),
            P(),
            P("dp", "tensor"),
            P("dp", "tensor", None),
            P("dp", "tensor"),
            P("dp", "tensor"),
            P("tensor", "dp"),
            P("tensor", "dp"),
            P(("groups", "dp"), None, None, None),
            P(("groups", "dp"), None, None, None),
            P(("groups", "dp")),
            P(("groups", "dp")),
        ),
        out_specs=P(("groups", "tensor"), "dp"),
        check_vma=False,
    )
```

profile of v0, /device:TPU:0, one launch (start us, length us, event | category | flops | bytes accessed | tf_op | source)
XLA Modules:
  0.0 433.0 jit_solution(11441684999754746054)
XLA Ops:
  6.5 2.2 convert_reduce_fusion
  8.8 0.2 copy-done.1
  9.0 2.8 multiply_reduce_fusion
  11.8 0.8 dynamic-slice.2
  12.6 2.3 fusion.1
  14.8 0.0 all-gather.2.cloned.1.call-update
  14.9 0.0 all-reduce.3.cloned.1.call-start
  14.9 53.3 %all-gather.2.cloned.1.call-done = bf16[768,1536]{1,0:T(8,128)(2,1)} async-done(((bf16[192,1536]{1,0:T(8,128)(2,1)}), bf16[768,1536]{1,0:T(8,128)(2,1)}) %all-gather.2.cloned.1.call-update) | async-done | bytes 2359312 | tf_op jit(solution)/shard_map/all_gather | solution.py:62
  68.2 4.0 fusion.6
  72.2 0.0 all-reduce.3.cloned.1.call-update
  72.2 0.0 reduce-scatter.4.cloned.1.call-start
  72.3 2.8 fusion.49
  75.1 2.5 fusion.51
  77.6 1.1 fusion.50
  78.7 1.7 pad_maximum_fusion
  80.5 3.5 copy.33
  84.0 0.0 all-reduce.5.cloned.1.call-start
  85.4 89.3 %all-reduce.3.cloned.1.call-done = f32[768,1024]{1,0:T(8,128)} async-done(((f32[768,1024]{1,0:T(8,128)}), f32[768,1024]{1,0:T(8,128)}) %all-reduce.3.cloned.1.call-update) | async-done | bytes 3145744 | tf_op jit(solution)/shard_map/psum | solution.py:67
  174.7 1.7 dynamic_slice.30
  176.3 1.6 copy.28
  178.0 1.6 reshape.177
  179.6 32.3 %reduce-scatter.4.cloned.1.call-done = f32[192,896]{1,0:T(8,128)} async-done(((f32[768,896]{1,0:T(8,128)}), f32[192,896]{1,0:T(8,128)}) %reduce-scatter.4.cloned.1.call-update) | async-done | bytes 688144
  211.9 1.5 slice.36
  213.4 1.6 copy.35
  215.1 1.6 reshape.176
  216.7 1.9 fusion.44
  218.6 1.9 copy.40
  220.5 1.9 copy.41
  222.3 1.3 fusion.45
  223.7 1.0 fusion.30
  224.6 0.6 copy-done.4
  225.3 0.7 copy.27
  226.0 1.5 convert_element_type.51
  227.5 1.1 fusion.48
  228.5 1.2 fusion.47
  229.7 0.1 fusion.13
  229.8 0.2 fusion.12
  230.0 1.1 fusion.16
  231.1 1.8 fusion.5
  232.9 1.5 copy.31
  234.4 1.2 multiply_convert_fusion
  235.6 1.6 pad_maximum_fusion.1
  237.2 1.7 copy.32
  239.0 8.4 %all_gather.7 = bf16[768,512]{1,0:T(8,128)(2,1)S(1)} all-gather(bf16[192,512]{1,0:T(8,128)(2,1)} %copy.32), channel_id=1, replica_groups=mesh['groups'=2,'tensor'=4,'dp'=4] {'dp'}, dimensions={0}, use_global_device_ids=true | all-gather | bytes 983040 | tf_op jit(solution)/shard_map/all_gather | solution.py:118
  247.4 1.4 fusion.8
  248.8 2.9 convolution_add_fusion
  251.7 172.5 %all-reduce.5.cloned.1.call-done = f32[768,1536]{1,0:T(8,128)} async-done(((f32[768,1536]{1,0:T(8,128)}), f32[768,1536]{1,0:T(8,128)}) %all-reduce.5.cloned.1.call-update) | async-done | bytes 4718608 | tf_op jit(solution)/shard_map/psum | solution.py:126
  424.2 2.2 add_convert_fusion
  (23 shorter events, 0.1 us)
Async XLA Ops:
  6.5 240.8 %copy-start = (bf16[384,1536]{1,0:T(8,128)(2,1)S(1)}, bf16[384,1536]{1,0:T(8,128)(2,1)}, u32[]{:S(2)}) copy-start(bf16[384,1536]{1,0:T(8,128)(2,1)} %param.19) | copy-start | bytes 3538948
  6.5 2.5 copy-start.1
  6.5 61.7 %all-gather.2.cloned.1.call-start = ((), (), s32[]{:S(2)}) async-start(), calls=%async_computation.1 | async-start | bytes 2949120 | tf_op jit(solution)/shard_map/all_gather | solution.py:62
  14.9 159.8 %all-reduce.3.cloned.1.call-start = ((), (), s32[]{:S(2)}) async-start(), calls=%async_computation.2 | async-start | bytes 6291456 | tf_op jit(solution)/shard_map/psum | solution.py:67
  72.2 139.7 %reduce-scatter.4.cloned.1.call-start = ((), (), s32[]{:S(2)}) async-start(), calls=%async_computation.4 | async-start | bytes 3440640
  72.3 2.8 copy-start.2
  75.1 2.5 copy-start.6
  84.0 340.3 %all-reduce.5.cloned.1.call-start = ((), (), s32[]{:S(2)}) async-start(), calls=%async_computation.3 | async-start | bytes 9437184 | tf_op jit(solution)/shard_map/psum | solution.py:126
  224.6 0.6 copy-start.4
  224.6 0.6 copy-start.5
  247.4 1.4 copy-start.3
Sparse Core Ops, SparseCore 0:
  15.0 53.1 all-gather.1
  72.4 102.2 all-reduce.2
  177.2 34.6 reduce-scatter.3
  251.8 172.3 all-reduce.4
where the time goes:
time: 434 us; the launch traced here: 433 us
  waiting for transfers between devices  347 us (80%)
  local copies, waits for them, and re-layouts  27.3 us (6%)
  matrix products  19.8 us (5%)
  other arithmetic  15.3 us (4%)
  between operations  14.6 us (3%)
  blocking collectives  8.4 us (2%)
    psum x1, waiting for transfers between devices, on_device(): summed = lax.psum(partial_terms, 'tensor')  172 us
    psum x1, waiting for transfers between devices, on_device(): keyval = lax.psum(kv_term, ('tensor', 'dp'))  89.3 us
    all_gather x1, waiting for transfers between devices, on_device(): every_row = lax.all_gather(own_block, 'tensor', axis=0, tiled=True)  53.3 us
    unnamed x5, waiting for transfers between devices  32.4 us
    unnamed x18, local copies, waits for them, and re-layouts  9.7 us
  transfers between devices with their start and end apart: 4, of which 4 were waited for; matrix products, arithmetic and copies ran while one was open for 4% of the time, Pallas kernels for 0%

commit v1 on v0

--- a/solution.py
+++ b/solution.py
@@ -1,6 +1,10 @@
+import functools
+
 import jax
 import jax.numpy as jnp
 from jax import lax
+from jax.experimental import pallas as pl
+from jax.experimental.pallas import tpu as pltpu
 from jax.sharding import PartitionSpec as P
 
 SPAN = 192
@@ -127,10 +131,491 @@
     own_sum = lax.dynamic_slice_in_dim(summed, tensor_index * row_share, row_share, 0)
     return (residual + own_sum).astype(jnp.bfloat16)
 
+GATHER_CHUNKS = 2
+REDUCE_CHUNKS = 4
+
+
+def fused_kernel(
+    sizes,
+    x_hbm,
+    gain_ref,
+    wq_hbm,
+    wkv_hbm,
+    wg_hbm,
+    wu_hbm,
+    wo_hbm,
+    wd_hbm,
+    ck_hbm,
+    cv_hbm,
+    cos_ref,
+    sin_ref,
+    bias_ref,
+    out_ref,
+    x_buf,
+    rows_buf,
+    w_in,
+    wo_buf,
+    wd_buf,
+    ck_buf,
+    cv_buf,
+    part_send,
+    part_own,
+    part_recv,
+    att_buf,
+    hid_buf,
+    acc,
+    from_left,
+    from_right,
+    sum_send,
+    x_sem,
+    load_sem,
+    kv_send,
+    kv_recv,
+    row_send_l,
+    row_send_r,
+    row_recv,
+    part_ssem,
+    part_rsem,
+    joined_ssem,
+    joined_rsem,
+    sum_ssem,
+    left_rsem,
+    right_rsem,
+):
+    n, span, head, ffn, block, sub = sizes
+    t = lax.axis_index("tensor")
+    d = lax.axis_index("dp")
+    mesh_id = pl.DeviceIdType.MESH
+    last = n - 1
+    ga = span // GATHER_CHUNKS
+    ra = span // REDUCE_CHUNKS
+    own_cols = pl.ds(pl.multiple_of(d * block, 128), block)
+
+    def rows_of(chunk, size):
+        return pl.ds(pl.multiple_of(chunk * size, size), size)
+
+    def remote(src, dst, ssem, rsem, axis, index):
+        return pltpu.make_async_remote_copy(
+            src_ref=src,
+            dst_ref=dst,
+            send_sem=ssem,
+            recv_sem=rsem,
+            device_id={axis: index},
+            device_id_type=mesh_id,
+        )
+
+    def x_copy(chunk):
+        rows = rows_of(chunk, ga)
+        return pltpu.make_async_copy(x_hbm.at[rows], x_buf.at[rows], x_sem.at[chunk])
+
+    own_sub = pl.ds(pl.multiple_of(t * sub, sub), sub)
+    key_cols = pl.ds(pl.multiple_of(t * head, head), head)
+    value_cols = pl.ds(pl.multiple_of((n + t) * head, head), head)
+    gate_at = 3 * head
+    up_at = 3 * head + ffn
+    loads = [
+        (wq_hbm, w_in.at[:, pl.ds(0, head)]),
+        (wg_hbm, w_in.at[:, pl.ds(gate_at, ffn)]),
+        (wu_hbm, w_in.at[:, pl.ds(up_at, ffn)]),
+        (wkv_hbm.at[:, key_cols], w_in.at[own_sub, pl.ds(head, head)]),
+        (wkv_hbm.at[:, value_cols], w_in.at[own_sub, pl.ds(2 * head, head)]),
+        (wo_hbm, wo_buf),
+        (wd_hbm, wd_buf),
+        (ck_hbm.at[t], ck_buf),
+        (cv_hbm.at[t], cv_buf),
+    ]
+    load_copies = [
+        pltpu.make_async_copy(a, b, load_sem.at[i]) for i, (a, b) in enumerate(loads)
+    ]
+
+    def kv_copy(peer, kind, slot):
+        cols = pl.ds(pl.multiple_of((kind * n + peer) * head, head), head)
+        return remote(
+            wkv_hbm.at[:, cols],
+            w_in.at[own_sub, pl.ds((1 + kind) * head, head)],
+            kv_send.at[slot, kind],
+            kv_recv.at[t, kind],
+            "tensor",
+            peer,
+        )
+
+    def kv_arrival(peer, kind):
+        rows = pl.ds(pl.multiple_of(peer * sub, sub), sub)
+        dst = w_in.at[rows, pl.ds((1 + kind) * head, head)]
+        return remote(dst, dst, kv_send.at[0, kind], kv_recv.at[peer, kind], "tensor", peer)
+
+    def row_copy(s, chunk, to_left):
+        view = rows_buf.at[s, rows_of(chunk, ga)]
+        sems = row_send_l if to_left else row_send_r
+        target = t - 1 if to_left else t + 1
+        return remote(view, view, sems.at[s, chunk], row_recv.at[s, chunk], "tensor", target)
+
+    def part_copy(s, chunk):
+        rows = rows_of(chunk, ga)
+        return remote(
+            part_send.at[s, rows],
+            part_recv.at[d, rows],
+            part_ssem.at[s, chunk],
+            part_rsem.at[d, chunk],
+            "dp",
+            s,
+        )
+
+    def part_arrival(peer, chunk):
+        dst = part_recv.at[peer, rows_of(chunk, ga)]
+        return remote(
+            dst, dst, part_ssem.at[peer, chunk], part_rsem.at[peer, chunk], "dp", peer
+        )
+
+    def joined_copy(s, peer, slot, kind):
+        view = (att_buf if kind else hid_buf).at[s]
+        return remote(
+            view, view, joined_ssem.at[slot, kind], joined_rsem.at[s, kind], "dp", peer
+        )
+
+    def sum_copy(s, chunk, to_left):
+        rows = rows_of(chunk, ra)
+        dst = (from_right if to_left else from_left).at[s, rows]
+        sems = right_rsem if to_left else left_rsem
+        target = t - 1 if to_left else t + 1
+        return remote(
+            sum_send.at[s, rows], dst, sum_ssem.at[s, chunk], sems.at[s, chunk], "tensor", target
+        )
+
+    for chunk in range(GATHER_CHUNKS):
+        x_copy(chunk).start()
+    for copy in load_copies:
+        copy.start()
+
+    barrier = pltpu.get_barrier_semaphore()
+    for p in range(1, n):
+        pl.semaphore_signal(
+            barrier, inc=1, device_id={"tensor": lax.rem(t + p, n)}, device_id_type=mesh_id
+        )
+        pl.semaphore_signal(
+            barrier, inc=1, device_id={"dp": lax.rem(d + p, n)}, device_id_type=mesh_id
+        )
+    pl.semaphore_wait(barrier, 2 * (n - 1))
+
+    for p in range(1, n):
+        for kind in range(2):
+            kv_copy(lax.rem(t + p, n), kind, p).start()
+
+    norm_rows = 16
+    gain = gain_ref[:, own_cols]
+
+    @pl.loop(0, GATHER_CHUNKS)
+    def _(chunk):
+        x_copy(chunk).wait()
+
+        @pl.loop(0, ga // norm_rows)
+        def _(i):
+            rows = pl.ds(pl.multiple_of(chunk * ga + i * norm_rows, norm_rows), norm_rows)
+            wide = x_buf[rows, :].astype(jnp.float32)
+            mean = jnp.mean(wide, axis=-1, keepdims=True)
+            centered = wide - mean
+            spread = jnp.mean(centered * centered, axis=-1, keepdims=True)
+            own = x_buf[rows, own_cols].astype(jnp.float32) - mean
+            normed = (own * lax.rsqrt(spread + norm_eps) * gain).astype(jnp.bfloat16)
+            rows_buf[t, rows, :] = normed
+
+        @pl.when(t > 0)
+        def _():
+            row_copy(t, chunk, True).start()
+
+        @pl.when(t < last)
+        def _():
+            row_copy(t, chunk, False).start()
+
+    for copy in load_copies:
+        copy.wait()
+    for p in range(1, n):
+        for kind in range(2):
+            kv_arrival(lax.rem(t + p, n), kind).wait_recv()
+
+    inner = jnp.where((t > 0) & (t < last), 1, 0)
+    near = jnp.where(t < 2, 1, 0)
+
+    def mirrored(v):
+        return near * v + (1 - near) * (last - v)
+
+    def rotated(v):
+        lane = lax.broadcasted_iota(jnp.int32, v.shape, 1)
+        swapped = jnp.where(
+            lax.rem(lane, 2) == 0, pltpu.roll(v, head - 1, 1), pltpu.roll(v, 1, 1)
+        )
+        return v * cos_ref[...] + swapped * sin_ref[...]
+
+    def attend(s):
+        for p in range(1, n):
+            peer = lax.rem(d + p, n)
+            for chunk in range(GATHER_CHUNKS):
+                part_arrival(peer, chunk).wait_recv()
+
+        def total(first, width):
+            cols = pl.ds(first, width)
+            result = part_own[:, cols]
+            for p in range(1, n):
+                result = result + part_recv[lax.rem(d + p, n), :, cols].astype(jnp.float32)
+            return result
+
+        gate = total(gate_at, ffn)
+        up = total(up_at, ffn)
+        hid_buf[s] = (gate / (1.0 + jnp.exp(-gate)) * up).astype(jnp.bfloat16)
+        for p in range(1, n):
+            joined_copy(s, lax.rem(d + p, n), p, 0).start()
+        query = rotated(total(0, head)).astype(jnp.bfloat16)
+        new_keys = rotated(total(head, head)).astype(jnp.bfloat16)
+        new_values = total(2 * head, head).astype(jnp.bfloat16)
+        scale = head ** (-0.5)
+        contract = (((1,), (1,)), ((), ()))
+        cached = (
+            lax.dot_general(query, ck_buf[...], contract, preferred_element_type=jnp.float32)
+            * scale
+            + bias_ref[...]
+        )
+        fresh = (
+            lax.dot_general(query, new_keys, contract, preferred_element_type=jnp.float32) * scale
+        )
+        row_at = lax.broadcasted_iota(jnp.int32, (span, span), 0)
+        col_at = lax.broadcasted_iota(jnp.int32, (span, span), 1)
+        fresh = jnp.where(row_at >= col_at, fresh, -jnp.inf)
+        peak = jnp.maximum(
+            jnp.max(cached, axis=-1, keepdims=True), jnp.max(fresh, axis=-1, keepdims=True)
+        )
+        cached_exp = jnp.exp(cached - peak)
+        fresh_exp = jnp.exp(fresh - peak)
+        denominator = jnp.sum(cached_exp, axis=-1, keepdims=True) + jnp.sum(
+            fresh_exp, axis=-1, keepdims=True
+        )
+        cached_prob = (cached_exp / denominator).astype(jnp.bfloat16)
+        fresh_prob = (fresh_exp / denominator).astype(jnp.bfloat16)
+        att_buf[s] = (
+            jnp.dot(cached_prob, cv_buf[...], preferred_element_type=jnp.float32)
+            + jnp.dot(fresh_prob, new_values, preferred_element_type=jnp.float32)
+        ).astype(jnp.bfloat16)
+        for p in range(1, n):
+            joined_copy(s, lax.rem(d + p, n), p, 1).start()
+
+    def project(s):
+        @pl.loop(0, GATHER_CHUNKS)
+        def _(chunk):
+            @pl.when(s != t)
+            def _():
+                row_copy(s, chunk, True).wait_recv()
+
+            @pl.when((s < t) & (t < last))
+            def _():
+                row_copy(s, chunk, False).start()
+
+            @pl.when((s > t) & (t > 0))
+            def _():
+                row_copy(s, chunk, True).start()
+
+            rows = rows_of(chunk, ga)
+            term = jnp.dot(rows_buf[s, rows, :], w_in[...], preferred_element_type=jnp.float32)
+
+            @pl.when(s == d)
+            def _():
+                part_own[rows, :] = term
+
+            @pl.when(s != d)
+            def _():
+                part_send[s, rows, :] = term.astype(jnp.bfloat16)
+                part_copy(s, chunk).start()
+
+        @pl.when(s == d)
+        def _():
+            attend(s)
+
+    col_tile = 512
+
+    def combine(s):
+        @pl.when(s != d)
+        def _():
+            joined_copy(s, s, 1, 0).wait_recv()
+            joined_copy(s, s, 1, 1).wait_recv()
+
+        @pl.loop(0, block // col_tile)
+        def _(i):
+            cols = pl.ds(pl.multiple_of(i * col_tile, col_tile), col_tile)
+            acc[:, cols] = jnp.dot(
+                att_buf[s], wo_buf[:, cols], preferred_element_type=jnp.float32
+            ) + jnp.dot(hid_buf[s], wd_buf[:, cols], preferred_element_type=jnp.float32)
+
+        @pl.loop(0, REDUCE_CHUNKS)
+        def _(chunk):
+            rows = rows_of(chunk, ra)
+
+            @pl.when((t > 0) & (t <= s))
+            def _():
+                sum_copy(s, chunk, False).wait_recv()
+                acc[rows, :] += from_left[s, rows, :].astype(jnp.float32)
+
+            @pl.when((t < last) & (t >= s))
+            def _():
+                sum_copy(s, chunk, True).wait_recv()
+                acc[rows, :] += from_right[s, rows, :].astype(jnp.float32)
+
+            @pl.when(t == s)
+            def _():
+                residual = x_buf[rows, own_cols].astype(jnp.float32)
+                out_ref[rows, :] = (residual + acc[rows, :]).astype(jnp.bfloat16)
+
+            @pl.when(t != s)
+            def _():
+                sum_send[s, rows, :] = acc[rows, :].astype(jnp.bfloat16)
+
+            @pl.when(t < s)
+            def _():
+                sum_copy(s, chunk, False).start()
+
+            @pl.when(t > s)
+            def _():
+                sum_copy(s, chunk, True).start()
+
+    @pl.loop(0, 2 * n)
+    def _(slot):
+        outer_p = (slot < 3) | (slot == 5)
+        inner_p = slot < 4
+        is_p = jnp.where(inner == 1, jnp.where(inner_p, 1, 0), jnp.where(outer_p, 1, 0))
+        event_p = jnp.where(slot < 4, slot, 3)
+        event_c = jnp.where(inner == 1, slot - 4, jnp.where(slot < 5, slot - 3, slot - 4))
+
+        @pl.when(is_p == 1)
+        def _():
+            swapped = jnp.where((inner == 1) & (event_p < 2), 1 - event_p, event_p)
+            project(mirrored(swapped))
+
+        @pl.when(is_p == 0)
+        def _():
+            ends = lax.rem(event_c + 1, n)
+            middle = jnp.where(event_c < 2, 2 - event_c, jnp.where(event_c == 2, 3, 0))
+            combine(mirrored(jnp.where(inner == 1, middle, ends)))
+
+    for p in range(1, n):
+        peer_t = lax.rem(t + p, n)
+        peer_d = lax.rem(d + p, n)
+        for kind in range(2):
+            kv_copy(peer_t, kind, p).wait_send()
+            joined_copy(d, peer_d, p, kind).wait_send()
+        for chunk in range(GATHER_CHUNKS):
+            part_copy(peer_d, chunk).wait_send()
+
+    @pl.loop(0, n)
+    def _(s):
+        for chunk in range(GATHER_CHUNKS):
+            @pl.when((s >= t) & (t > 0))
+            def _():
+                row_copy(s, chunk, True).wait_send()
+
+            @pl.when((s <= t) & (t < last))
+            def _():
+                row_copy(s, chunk, False).wait_send()
+
+        for chunk in range(REDUCE_CHUNKS):
+            @pl.when(t < s)
+            def _():
+                sum_copy(s, chunk, False).wait_send()
+
+            @pl.when(t > s)
+            def _():
+                sum_copy(s, chunk, True).wait_send()
+
+
+def fused_on_device(
+    inputs,
+    ln_gain,
+    w_query,
+    w_keyval,
+    w_gate,
+    w_up,
+    w_out,
+    w_down,
+    cache_keys,
+    cache_values,
+    lengths,
+    starts,
+):
+    n = lax.axis_size("tensor")
+    block, head = w_query.shape
+    ffn = w_gate.shape[1]
+    sub = w_keyval.shape[1]
+    cache = cache_keys.shape[2]
+    width = 3 * head + 2 * ffn
+    lane = jnp.arange(head, dtype=jnp.int32)
+    pair = (lane // 2).astype(jnp.float32)
+    frequency = rope_base ** (-2.0 * pair / head)
+    positions = (starts[0] + jnp.arange(SPAN, dtype=jnp.int32)).astype(jnp.float32)
+    angles = positions[:, None] * frequency
+    cosine = jnp.cos(angles)
+    sine = jnp.sin(angles) * jnp.where(lane % 2 == 0, -1.0, 1.0)
+    bias = jnp.where(jnp.arange(cache) < lengths[0], 0.0, -jnp.inf).astype(jnp.float32)
+    bf16, f32 = jnp.bfloat16, jnp.float32
+    anywhere = pl.BlockSpec(memory_space=pl.ANY)
+    vmem = pl.BlockSpec(memory_space=pltpu.VMEM)
+    dma = pltpu.SemaphoreType.DMA
+    return pl.pallas_call(
+        functools.partial(fused_kernel, (n, SPAN, head, ffn, block, sub)),
+        out_shape=jax.ShapeDtypeStruct((SPAN, block), bf16),
+        in_specs=[anywhere, vmem] + [anywhere] * 8 + [vmem] * 3,
+        out_specs=vmem,
+        scratch_shapes=[
+            pltpu.VMEM(inputs.shape, bf16),
+            pltpu.VMEM((n, SPAN, block), bf16),
+            pltpu.VMEM((block, width), bf16),
+            pltpu.VMEM(w_out.shape, bf16),
+            pltpu.VMEM(w_down.shape, bf16),
+            pltpu.VMEM((cache, head), bf16),
+            pltpu.VMEM((cache, head), bf16),
+            pltpu.VMEM((n, SPAN, width), bf16),
+            pltpu.VMEM((SPAN, width), f32),
+            pltpu.VMEM((n, SPAN, width), bf16),
+            pltpu.VMEM((n, SPAN, head), bf16),
+            pltpu.VMEM((n, SPAN, ffn), bf16),
+            pltpu.VMEM((SPAN, block), f32),
+            pltpu.VMEM((n, SPAN, block), bf16),
+            pltpu.VMEM((n, SPAN, block), bf16),
+            pltpu.VMEM((n, SPAN, block), bf16),
+            dma((GATHER_CHUNKS,)),
+            dma((9,)),
+            dma((n, 2)),
+            dma((n, 2)),
+            dma((n, GATHER_CHUNKS)),
+            dma((n, GATHER_CHUNKS)),
+            dma((n, GATHER_CHUNKS)),
+            dma((n, GATHER_CHUNKS)),
+            dma((n, GATHER_CHUNKS)),
+            dma((n, 2)),
+            dma((n, 2)),
+            dma((n, REDUCE_CHUNKS)),
+            dma((n, REDUCE_CHUNKS)),
+            dma((n, REDUCE_CHUNKS)),
+        ],
+        compiler_params=pltpu.CompilerParams(
+            collective_id=0, has_side_effects=True, vmem_limit_bytes=48 * 1024 * 1024
+        ),
+    )(
+        inputs,
+        ln_gain[None, :],
+        w_query,
+        w_keyval[0],
+        w_gate,
+        w_up,
+        w_out,
+        w_down,
+        cache_keys[0],
+        cache_values[0],
+        cosine,
+        sine,
+        bias[None, :],
+    )
+
 
 def solution(mesh):
+    fits = mesh.shape["tensor"] == mesh.shape["dp"] == 4
     return jax.shard_map(
-        on_device,
+        fused_on_device if fits else on_device,
         mesh=mesh,
         in_specs=(
             P(("groups", "tensor"), None),

time: 434 us -> 136 us (0.31)
  waiting for transfers between devices: 347 us -> 0 us
  Pallas kernels: 0 us -> 125 us
  matrix products: 19.8 us -> 0 us
  local copies, waits for them, and re-layouts: 27.3 us -> 9.11 us
  other arithmetic: 15.3 us -> 0.44 us
  between operations: 14.6 us -> 1.35 us
  blocking collectives: 8.4 us -> 0 us
    psum x2 -> x0, waiting for transfers between devices: 262 us -> none  [the longest x1 172 us: on_device(): summed = lax.psum(partial_terms, 'tensor')]
    pallas_call x0 -> x1, Pallas kernels: none -> 125 us  [fused_on_device(): pl.pallas_call(functools.partial(fused_kernel, (n, SPAN, head, ffn, block...]
    all_gather x1 -> x0, waiting for transfers between devices: 53.3 us -> none  [on_device(): every_row = lax.all_gather(own_block, 'tensor', axis=0, tiled=True)]
    unnamed x5 -> x0, waiting for transfers between devices: 32.4 us -> none
    dot_general x10 -> x0, matrix products: 19.8 us -> none  [the longest x1 4 us: on_device(): kv_term = jnp.dot(kv_rows, w_keyval[0], preferred_element_type=jnp.float32)]
    all_gather x1 -> x0, blocking collectives: 8.4 us -> none  [on_device(): gathered_piece = lax.all_gather(joined, 'dp', axis=0, tiled=True)]
    convert_element_type x4 -> x1, other arithmetic: 5.69 us -> 0.01 us  [fused_on_device(): (starts[0] + jnp.arange(SPAN, dtype=jnp.int32)).astype(jnp.float32)]
    reduce_sum x4 -> x0, other arithmetic: 5.27 us -> none  [the longest x1 2.79 us: layer_norm(): spread_sq = jnp.mean(centered * centered, axis=-1, keepdims=True)]
  transfers between devices with their start and end apart: 4 -> 0, of which waited for: 4 -> 0; matrix products, arithmetic and copies ran while one was open for 4% -> 0% of each run, Pallas kernels for 0% -> 0%
where the time goes in v1:
time: 136 us
  Pallas kernels  125 us (92%)
  local copies, waits for them, and re-layouts  9.11 us (7%)
    pallas_call x1, Pallas kernels, fused_on_device(): pl.pallas_call(functools.partial(fused_kernel, (n, SPAN, head, ffn, block...  125 us
    unnamed x17, local copies, waits for them, and re-layouts  9.11 us

profile of v1, /device:TPU:0, one launch (start us, length us, event | category | flops | bytes accessed | tf_op | source)
XLA Modules:
  0.0 135.8 jit_solution(16932554042548045515)
XLA Ops:
  1.3 0.4 fusion
  1.8 0.0 copy-start
  1.8 1.3 copy-done
  3.0 0.0 copy-start.1
  3.0 1.3 copy-done.1
  4.3 0.0 copy-start.2
  4.3 1.1 copy-done.2
  5.4 0.0 copy-start.3
  5.4 1.0 copy-done.3
  6.4 0.0 copy-start.4
  6.4 1.0 copy-done.4
  7.4 0.0 copy-start.5
  7.4 0.9 copy-done.5
  8.4 0.0 copy-start.6
  8.4 0.9 copy-done.6
  9.3 0.0 copy-start.7
  9.3 0.7 copy-done.7
  10.1 124.9 %shard_map.118 = bf16[192,1536]{1,0:T(8,128)(2,1)S(1)} custom-call(bf16[192,6144]{1,0:T(8,128)(2,1)} %x_hbm.1, f32[1,6144]{1,0:T(1,128)S(1)} %bitcast.11, bf16[1536,128]{1,0:T(8,128)(2,1)S(1)} %copy-done.3, bf16[384,1024]{1,0:T(8,128)(2,1)S(1)} %bitcast.8, bf16[1536,384]{1,0:T(8,128)(2,1)S(1)} %copy-done, bf16[1536,384]{1,0:T(8,128)(2,1)S(1)} %copy-done.1, ...), custom_call_target="tpu_custom_call" | custom-call | tf_op jit(solution)/shard_map/pallas_call | solution.py:558
  135.0 0.8 copy.16
  (3 shorter events, 0.0 us)
Async XLA Ops:
  1.8 1.3 copy-start
  3.0 1.3 copy-start.1
  4.3 1.1 copy-start.2
  5.4 1.0 copy-start.3
  6.4 1.0 copy-start.4
  7.4 0.9 copy-start.5
  8.4 0.9 copy-start.6
  9.3 0.7 copy-start.7

commit v2 on v1

--- a/solution.py
+++ b/solution.py
@@ -132,7 +132,8 @@
     return (residual + own_sum).astype(jnp.bfloat16)
 
 GATHER_CHUNKS = 2
-REDUCE_CHUNKS = 4
+REDUCE_CHUNKS = 6
+LEAD = 3
 
 
 def fused_kernel(
@@ -171,6 +172,8 @@
     load_sem,
     kv_send,
     kv_recv,
+    share_send,
+    share_recv,
     row_send_l,
     row_send_r,
     row_recv,
@@ -185,6 +188,7 @@
     n, span, head, ffn, block, sub = sizes
     t = lax.axis_index("tensor")
     d = lax.axis_index("dp")
+    g = lax.axis_index("groups")
     mesh_id = pl.DeviceIdType.MESH
     last = n - 1
     ga = span // GATHER_CHUNKS
@@ -228,11 +232,18 @@
         pltpu.make_async_copy(a, b, load_sem.at[i]) for i, (a, b) in enumerate(loads)
     ]
 
+    half = sub // 2
+
+    def kv_part(owner, kind, group):
+        rows = pl.ds(pl.multiple_of(owner * sub + group * half, half), half)
+        return w_in.at[rows, pl.ds((1 + kind) * head, head)]
+
     def kv_copy(peer, kind, slot):
         cols = pl.ds(pl.multiple_of((kind * n + peer) * head, head), head)
+        rows = pl.ds(pl.multiple_of(g * half, half), half)
         return remote(
-            wkv_hbm.at[:, cols],
-            w_in.at[own_sub, pl.ds((1 + kind) * head, head)],
+            wkv_hbm.at[rows, cols],
+            kv_part(t, kind, g),
             kv_send.at[slot, kind],
             kv_recv.at[t, kind],
             "tensor",
@@ -240,9 +251,20 @@
         )
 
     def kv_arrival(peer, kind):
-        rows = pl.ds(pl.multiple_of(peer * sub, sub), sub)
-        dst = w_in.at[rows, pl.ds((1 + kind) * head, head)]
+        dst = kv_part(peer, kind, g)
         return remote(dst, dst, kv_send.at[0, kind], kv_recv.at[peer, kind], "tensor", peer)
+
+    def kv_share(peer, kind, slot):
+        view = kv_part(peer, kind, g)
+        return remote(
+            view, view, share_send.at[slot, kind], share_recv.at[peer, kind], "groups", 1 - g
+        )
+
+    def kv_shared(peer, kind):
+        dst = kv_part(peer, kind, 1 - g)
+        return remote(
+            dst, dst, share_send.at[0, kind], share_recv.at[peer, kind], "groups", 1 - g
+        )
 
     def row_copy(s, chunk, to_left):
         view = rows_buf.at[s, rows_of(chunk, ga)]
@@ -295,7 +317,8 @@
         pl.semaphore_signal(
             barrier, inc=1, device_id={"dp": lax.rem(d + p, n)}, device_id_type=mesh_id
         )
-    pl.semaphore_wait(barrier, 2 * (n - 1))
+    pl.semaphore_signal(barrier, inc=1, device_id={"groups": 1 - g}, device_id_type=mesh_id)
+    pl.semaphore_wait(barrier, 2 * (n - 1) + 1)
 
     for p in range(1, n):
         for kind in range(2):
@@ -329,9 +352,17 @@
 
     for copy in load_copies:
         copy.wait()
-    for p in range(1, n):
-        for kind in range(2):
-            kv_arrival(lax.rem(t + p, n), kind).wait_recv()
+
+    def share_weights():
+        for p in range(1, n):
+            for kind in range(2):
+                kv_arrival(lax.rem(t + p, n), kind).wait_recv()
+                kv_share(lax.rem(t + p, n), kind, p).start()
+
+    def wait_weights():
+        for p in range(1, n):
+            for kind in range(2):
+                kv_shared(lax.rem(t + p, n), kind).wait_recv()
 
     inner = jnp.where((t > 0) & (t < last), 1, 0)
     near = jnp.where(t < 2, 1, 0)
@@ -397,21 +428,22 @@
         for p in range(1, n):
             joined_copy(s, lax.rem(d + p, n), p, 1).start()
 
+    def forward(s):
+        @pl.loop(0, GATHER_CHUNKS)
+        def _(chunk):
+            row_copy(s, chunk, True).wait_recv()
+
+            @pl.when((s < t) & (t < last))
+            def _():
+                row_copy(s, chunk, False).start()
+
+            @pl.when((s > t) & (t > 0))
+            def _():
+                row_copy(s, chunk, True).start()
+
     def project(s):
         @pl.loop(0, GATHER_CHUNKS)
         def _(chunk):
-            @pl.when(s != t)
-            def _():
-                row_copy(s, chunk, True).wait_recv()
-
-            @pl.when((s < t) & (t < last))
-            def _():
-                row_copy(s, chunk, False).start()
-
-            @pl.when((s > t) & (t > 0))
-            def _():
-                row_copy(s, chunk, True).start()
-
             rows = rows_of(chunk, ga)
             term = jnp.dot(rows_buf[s, rows, :], w_in[...], preferred_element_type=jnp.float32)
 
@@ -424,80 +456,158 @@
                 part_send[s, rows, :] = term.astype(jnp.bfloat16)
                 part_copy(s, chunk).start()
 
-        @pl.when(s == d)
-        def _():
-            attend(s)
-
     col_tile = 512
 
     def combine(s):
         @pl.when(s != d)
         def _():
             joined_copy(s, s, 1, 0).wait_recv()
-            joined_copy(s, s, 1, 1).wait_recv()
 
         @pl.loop(0, block // col_tile)
         def _(i):
             cols = pl.ds(pl.multiple_of(i * col_tile, col_tile), col_tile)
-            acc[:, cols] = jnp.dot(
+            acc[s, :, cols] = jnp.dot(
+                hid_buf[s], wd_buf[:, cols], preferred_element_type=jnp.float32
+            )
+
+        @pl.when(s != d)
+        def _():
+            joined_copy(s, s, 1, 1).wait_recv()
+
+        @pl.loop(0, block // col_tile)
+        def _(i):
+            cols = pl.ds(pl.multiple_of(i * col_tile, col_tile), col_tile)
+            acc[s, :, cols] += jnp.dot(
                 att_buf[s], wo_buf[:, cols], preferred_element_type=jnp.float32
-            ) + jnp.dot(hid_buf[s], wd_buf[:, cols], preferred_element_type=jnp.float32)
-
-        @pl.loop(0, REDUCE_CHUNKS)
-        def _(chunk):
-            rows = rows_of(chunk, ra)
-
-            @pl.when((t > 0) & (t <= s))
-            def _():
-                sum_copy(s, chunk, False).wait_recv()
-                acc[rows, :] += from_left[s, rows, :].astype(jnp.float32)
-
-            @pl.when((t < last) & (t >= s))
-            def _():
-                sum_copy(s, chunk, True).wait_recv()
-                acc[rows, :] += from_right[s, rows, :].astype(jnp.float32)
-
-            @pl.when(t == s)
-            def _():
-                residual = x_buf[rows, own_cols].astype(jnp.float32)
-                out_ref[rows, :] = (residual + acc[rows, :]).astype(jnp.bfloat16)
-
-            @pl.when(t != s)
-            def _():
-                sum_send[s, rows, :] = acc[rows, :].astype(jnp.bfloat16)
+            )
+
+    def pass_on(s, chunk):
+        rows = rows_of(chunk, ra)
+        place = (jnp.where(t < s, s - t, t - s) - 1) * REDUCE_CHUNKS + chunk
+
+        @pl.when((inner == 0) & (t != s) & (place >= 2))
+        def _():
+            far = (place - 2) // REDUCE_CHUNKS + 1
+            before = lax.rem(place - 2, REDUCE_CHUNKS)
 
             @pl.when(t < s)
             def _():
-                sum_copy(s, chunk, False).start()
+                sum_copy(t + far, before, False).wait_send()
 
             @pl.when(t > s)
             def _():
-                sum_copy(s, chunk, True).start()
-
-    @pl.loop(0, 2 * n)
+                sum_copy(t - far, before, True).wait_send()
+
+        @pl.when((t > 0) & (t <= s))
+        def _():
+            sum_copy(s, chunk, False).wait_recv()
+            acc[s, rows, :] += from_left[s, rows, :].astype(jnp.float32)
+
+        @pl.when((t < last) & (t >= s))
+        def _():
+            sum_copy(s, chunk, True).wait_recv()
+            acc[s, rows, :] += from_right[s, rows, :].astype(jnp.float32)
+
+        @pl.when(t == s)
+        def _():
+            residual = x_buf[rows, own_cols].astype(jnp.float32)
+            out_ref[rows, :] = (residual + acc[s, rows, :]).astype(jnp.bfloat16)
+
+        @pl.when(t != s)
+        def _():
+            sum_send[s, rows, :] = acc[s, rows, :].astype(jnp.bfloat16)
+
+        @pl.when(t < s)
+        def _():
+            sum_copy(s, chunk, False).start()
+
+        @pl.when(t > s)
+        def _():
+            sum_copy(s, chunk, True).start()
+
+    plans = (
+        "V0W0P0A0F1P1A1F2P2C0S0A2F3P3C1L1A3H1C2S2C3S3",
+        "V0F1F2W0P0A0P1P2F3A1A2P3A3C0C2C1S0C3D2D3S1N0",
+    )
+    plans = [[plan[i : i + 2] for i in range(0, len(plan), 2)] for plan in plans]
+    kinds = "PACSDLHFVWN"
+
+    def looked_up(slot, values):
+        found = 0
+        for i, pair in enumerate(zip(*values)):
+            picked = pair[0] if pair[0] == pair[1] else jnp.where(inner == 1, pair[1], pair[0])
+            found = jnp.where(slot == i, picked, found)
+        return found
+
+    p_order = ((0, 1, 2, 3), (1, 0, 2, 3))
+    c_order = ((1, 2, 3, 0), (2, 1, 3, 0))
+    step_kinds = [[kinds.index(step[0]) for step in plan] for plan in plans]
+    step_rows = [
+        [
+            (p_order if step[0] in "PAF" else c_order)[which][int(step[1])]
+            for step in plan
+        ]
+        for which, plan in enumerate(plans)
+    ]
+
+    @pl.loop(0, len(plans[0]))
     def _(slot):
-        outer_p = (slot < 3) | (slot == 5)
-        inner_p = slot < 4
-        is_p = jnp.where(inner == 1, jnp.where(inner_p, 1, 0), jnp.where(outer_p, 1, 0))
-        event_p = jnp.where(slot < 4, slot, 3)
-        event_c = jnp.where(inner == 1, slot - 4, jnp.where(slot < 5, slot - 3, slot - 4))
-
-        @pl.when(is_p == 1)
-        def _():
-            swapped = jnp.where((inner == 1) & (event_p < 2), 1 - event_p, event_p)
-            project(mirrored(swapped))
-
-        @pl.when(is_p == 0)
-        def _():
-            ends = lax.rem(event_c + 1, n)
-            middle = jnp.where(event_c < 2, 2 - event_c, jnp.where(event_c == 2, 3, 0))
-            combine(mirrored(jnp.where(inner == 1, middle, ends)))
+        kind = looked_up(slot, step_kinds)
+        s = mirrored(looked_up(slot, step_rows))
+
+        @pl.when(kind == 0)
+        def _():
+            project(s)
+
+        @pl.when((kind == 1) & (s == d))
+        def _():
+            attend(s)
+
+        @pl.when(kind == 2)
+        def _():
+            combine(s)
+
+        @pl.when(kind == 7)
+        def _():
+            forward(s)
+
+        @pl.when(kind == 8)
+        def _():
+            share_weights()
+
+        @pl.when(kind == 9)
+        def _():
+            wait_weights()
+
+        @pl.when((kind >= 3) & (kind <= 6))
+        def _():
+            first = mirrored(c_order[1][2])
+            second = mirrored(c_order[1][3])
+            late = jnp.where(s == second, 1, 0)
+            half_way = REDUCE_CHUNKS // 2
+            lead = min(LEAD, REDUCE_CHUNKS)
+            start = jnp.where(kind == 6, half_way, 0)
+            stop = jnp.where(kind == 5, half_way, REDUCE_CHUNKS)
+
+            @pl.loop(start, stop)
+            def _(i):
+                at = late * REDUCE_CHUNKS + i
+                mixed = at - lead
+                in_turns = (mixed >= 0) & (mixed < 2 * (REDUCE_CHUNKS - lead))
+                take_first = (mixed < 0) | (in_turns & (lax.rem(at + lead, 2) == 1))
+                later = jnp.where(take_first, lead + mixed // 2, mixed // 2)
+                chunk = jnp.where(
+                    in_turns, later, jnp.where(mixed < 0, at, at - REDUCE_CHUNKS)
+                )
+                turn = jnp.where(take_first, first, second)
+                pass_on(jnp.where(kind == 4, turn, s), jnp.where(kind == 4, chunk, i))
 
     for p in range(1, n):
         peer_t = lax.rem(t + p, n)
         peer_d = lax.rem(d + p, n)
         for kind in range(2):
             kv_copy(peer_t, kind, p).wait_send()
+            kv_share(peer_t, kind, p).wait_send()
             joined_copy(d, peer_d, p, kind).wait_send()
         for chunk in range(GATHER_CHUNKS):
             part_copy(peer_d, chunk).wait_send()
@@ -514,11 +624,13 @@
                 row_copy(s, chunk, False).wait_send()
 
         for chunk in range(REDUCE_CHUNKS):
-            @pl.when(t < s)
+            tail = chunk >= REDUCE_CHUNKS - 2
+
+            @pl.when((t < s) & ((inner == 1) | ((s - t == last) & tail)))
             def _():
                 sum_copy(s, chunk, False).wait_send()
 
-            @pl.when(t > s)
+            @pl.when((t > s) & ((inner == 1) | ((t - s == last) & tail)))
             def _():
                 sum_copy(s, chunk, True).wait_send()
 
@@ -573,12 +685,14 @@
             pltpu.VMEM((n, SPAN, width), bf16),
             pltpu.VMEM((n, SPAN, head), bf16),
             pltpu.VMEM((n, SPAN, ffn), bf16),
-            pltpu.VMEM((SPAN, block), f32),
+            pltpu.VMEM((n, SPAN, block), f32),
             pltpu.VMEM((n, SPAN, block), bf16),
             pltpu.VMEM((n, SPAN, block), bf16),
             pltpu.VMEM((n, SPAN, block), bf16),
             dma((GATHER_CHUNKS,)),
             dma((9,)),
+            dma((n, 2)),
+            dma((n, 2)),
             dma((n, 2)),
             dma((n, 2)),
             dma((n, GATHER_CHUNKS)),
@@ -593,7 +707,7 @@
             dma((n, REDUCE_CHUNKS)),
         ],
         compiler_params=pltpu.CompilerParams(
-            collective_id=0, has_side_effects=True, vmem_limit_bytes=48 * 1024 * 1024
+            collective_id=0, has_side_effects=True, vmem_limit_bytes=62 * 1024 * 1024
         ),
     )(
         inputs,
@@ -613,7 +727,7 @@
 
 
 def solution(mesh):
-    fits = mesh.shape["tensor"] == mesh.shape["dp"] == 4
+    fits = mesh.shape["tensor"] == mesh.shape["dp"] == 4 and mesh.shape["groups"] == 2
     return jax.shard_map(
         fused_on_device if fits else on_device,
         mesh=mesh,

time: 136 us -> 114 us (0.84); the launches traced: 136 us -> 112 us
  Pallas kernels: 125 us -> 107 us
  local copies, waits for them, and re-layouts: 9.11 us -> 1.92 us
    pallas_call x1, Pallas kernels: 125 us -> 107 us  [fused_on_device(): pl.pallas_call(functools.partial(fused_kernel, (n, SPAN, head, ffn, block...]
    unnamed x17 -> x1, local copies, waits for them, and re-layouts: 9.11 us -> 1.92 us
where the time goes in v2:
time: 114 us; the launch traced here: 112 us
  Pallas kernels  107 us (94%)
  local copies, waits for them, and re-layouts  1.92 us (2%)
  other arithmetic  1.67 us (1%)
  between operations  1.31 us (1%)
    pallas_call x1, Pallas kernels, fused_on_device(): pl.pallas_call(functools.partial(fused_kernel, (n, SPAN, head, ffn, block...  107 us

profile of v2, /device:TPU:0, one launch (start us, length us, event | category | flops | bytes accessed | tf_op | source)
XLA Modules:
  0.0 112.3 jit_solution(4855091558952998508)
XLA Ops:
  1.3 0.6 compare_select_fusion.bias_ref
  1.9 1.1 fusion
  3.0 107.4 %shard_map.118 = bf16[192,1536]{1,0:T(8,128)(2,1)} custom-call(bf16[192,6144]{1,0:T(8,128)(2,1)} %x_hbm.1, f32[1,6144]{1,0:T(1,128)} %bitcast.11, bf16[1536,128]{1,0:T(8,128)(2,1)} %wq_hbm.1, bf16[384,1024]{1,0:T(8,128)(2,1)} %bitcast.8, bf16[1536,384]{1,0:T(8,128)(2,1)} %wg_hbm.1, bf16[1536,384]{1,0:T(8,128)(2,1)} %wu_hbm.1, bf16[128,1536]{1,0:T(8,128)(2,1)} %wo_hbm.1, ...), custom_call_target="tpu_custom_call" | custom-call | tf_op jit(solution)/shard_map/pallas_call | solution.py:670
  110.4 1.9 %copy.16 = bf16[192,1536]{1,0:T(8,128)(2,1)} copy(bf16[192,1536]{1,0:T(8,128)(2,1)} %shard_map.118) | data formatting | bytes 1179648
  (2 shorter events, 0.0 us)
